TPU v7x, 32 devices: a whole 2x2x4 slice. The times are simulated.
32 devices in a mesh: depth: 8 (over z, y), tile: 4 (over x, core).
Axes of the slice: x: 2, y: 2, z: 4, core: 2. Of those that a mesh axis runs over, the one named last changes fastest.
Arguments:
- ensemble: bfloat16 [64, 8, 64, 8192], P('tile', None, 'depth'), may hold values from -8 to 8
- active: int32 [8, 64], P('depth'), may hold values from 0 to 1, as said below
- depth_rank: int32 [8], replicated, may hold values from 0 to 7, as said below
Outputs:
- picture: float32 [4, 4, 65536], P(None, 'tile', 'depth')
Inputs may be any that keep to these rules, and one draw needn't show every extreme that they name: Every slab has exactly 32 active bricks. depth_rank[s] = s XOR k for one integer k.
All inputs are finite; a program needn't handle non-finite values.
Results may differ from a plain program's by a relative error of at most 0.0003.
Values may be sent and summed in bfloat16 or wider, within the bound.
A program may use at most 128 MiB of HBM per device.

v0:
```python
import jax
import jax.numpy as jnp
from jax import lax
from jax.sharding import PartitionSpec as P

BZ = 2
SHARPNESS = 4.0
ISOVALUE = 0.25
DENSITY = 0.35


def swapped(x, axis, apart):
    return lax.ppermute(x, axis, [(i, i ^ 1 << apart) for i in range(lax.axis_size(axis))])


def illuminate(mean_field, variance, above_prob):
    spread = jnp.sqrt(variance + 1e-06)
    depth_sum = jnp.cumsum(above_prob, axis=-2)
    transmit = jnp.exp(-DENSITY * (depth_sum - above_prob))
    weight = transmit * (1.0 - jnp.exp(-DENSITY * above_prob))
    red_sum = jnp.sum(weight * jax.nn.sigmoid(2.0 * mean_field), axis=-2)
    green_sum = jnp.sum(weight * (spread / (1.0 + spread)), axis=-2)
    blue_sum = jnp.sum(weight * above_prob, axis=-2)
    opacity = 1.0 - jnp.exp(-DENSITY * depth_sum[..., -1, :])
    return jnp.stack([red_sum, green_sum, blue_sum, opacity])


def render_members(samples):
    mean_field = jnp.mean(samples, axis=0)
    variance = jnp.mean((samples - mean_field) ** 2, axis=0)
    above_prob = jnp.mean(jax.nn.sigmoid(SHARPNESS * (samples - ISOVALUE)), axis=0)
    return illuminate(mean_field, variance, above_prob)


def body(ensemble, active, depth_rank):
    tile_count = lax.axis_size("tile")
    tile_id = lax.axis_index("tile")
    depth_count = lax.axis_size("depth")
    depth_id = lax.axis_index("depth")
    cells = ensemble.shape[3]
    brick_total = active.shape[1]
    per_tile = brick_total // tile_count
    pixels = cells // BZ
    flag_row = active[0]
    own_flags = lax.dynamic_slice_in_dim(flag_row, tile_id * per_tile, per_tile).astype(jnp.float32)
    regrouped = lax.all_to_all(
        lax.all_to_all(ensemble, "depth", split_axis=1, concat_axis=2, tiled=True),
        "tile",
        split_axis=2,
        concat_axis=0,
        tiled=True,
    )
    samples = regrouped.astype(jnp.float32).reshape(regrouped.shape[0], per_tile, BZ, pixels)
    shaded = render_members(samples) * own_flags[None, :, None]
    block_len = per_tile * pixels // depth_count
    image_rows = shaded.reshape(4, depth_count, block_len)
    own_rank = depth_rank[depth_id]
    current = image_rows
    for section in range(depth_count.bit_length() - 1):
        paired = current.reshape(4, current.shape[1] // 2, 2, block_len)
        my_bit = depth_id >> section & 1
        kept = jnp.where(my_bit == 1, paired[:, :, 1], paired[:, :, 0])
        handed = jnp.where(my_bit == 1, paired[:, :, 0], paired[:, :, 1])
        partner = swapped(handed, "depth", section)
        partner_rank = depth_rank[depth_id ^ 1 << section]
        mine_front = own_rank < partner_rank
        front_part = jnp.where(mine_front, kept, partner)
        back_part = jnp.where(mine_front, partner, kept)
        current = front_part + (1.0 - front_part[3:4]) * back_part
    return current


def solution(mesh):
    in_specs = (P("tile", None, "depth", None), P("depth", None), P())
    out_specs = P(None, "tile", "depth")
    return jax.shard_map(body, mesh=mesh, in_specs=in_specs, out_specs=out_specs, check_vma=False)
```

profile of v0, /device:TPU:0, one launch (start us, length us, event | category | flops | bytes accessed | tf_op | source)
XLA Modules:
  0.0 664.0 jit_solution(898726807793159516)
XLA Ops:
  0.0 8.5 %copy.45 = bf16[16,8,8,8192]{3,2,0,1:T(8,128)(2,1)S(1)} copy(bf16[16,8,8,8192]{3,2,1,0:T(8,128)(2,1)} %param.3) | data formatting | bytes 33554432 | tf_op args[0]
  8.5 369.9 %all_to_all.21 = bf16[16,8,8,8192]{3,2,0,1:T(8,128)(2,1)S(1)} all-to-all(bf16[16,8,8,8192]{3,2,0,1:T(8,128)(2,1)S(1)} %copy.45), channel_id=1, replica_groups=mesh['depth'=8,'tile'=4] {'depth'}, dimensions={1} | all-to-all | bytes 33554432 | tf_op jit(solution)/shard_map/all_to_all | solution.py:47
  378.4 2.2 copy.77
  380.6 25.1 %copy.47 = bf16[16,1,64,8192]{3,0,1,2:T(8,128)(2,1)} copy(bf16[16,1,64,8192]{3,2,0,1:T(8,128)(2,1)S(1)} %bitcast.87) | data formatting | bytes 33554432 | tf_op jit(solution)/shard_map/all_to_all | solution.py:47
  405.8 7.1 %all-to-all-start.1 = ((bf16[16,1,64,8192]{3,0,1,2:T(8,128)(2,1)}), bf16[16,1,64,8192]{3,0,1,2:T(8,128)(2,1)}, u32[]{:S(2)}, u32[]{:S(2)}) async-start(bf16[16,1,64,8192]{3,0,1,2:T(8,128)(2,1)} %copy.47), calls=%async_computation.1 | async-start | bytes 33554432 | tf_op jit(solution)/shard_map/all_to_all | solution.py:46
  412.9 0.0 copy-done.1
  412.9 0.1 convert_reduce_fusion
  413.0 0.1 convert_element_type.29
  413.0 0.1 mul.110
  413.2 0.3 mul.111
  413.5 182.4 %all-to-all-done.1 = bf16[16,1,64,8192]{3,0,1,2:T(8,128)(2,1)} async-done(((bf16[16,1,64,8192]{3,0,1,2:T(8,128)(2,1)}), bf16[16,1,64,8192]{3,0,1,2:T(8,128)(2,1)}, u32[]{:S(2)}, u32[]{:S(2)}) %all-to-all-start.1) | async-done | bytes 16777248 | tf_op jit(solution)/shard_map/all_to_all | solution.py:46
  595.9 7.0 %fusion.1 = f32[16,8192]{1,0:T(8,128)S(1)} fusion(bf16[16,1,4,16,8192]{4,0,3,2,1:T(8,128)(2,1)} %bitcast.6), kind=kLoop, calls=%fused_computation.2 | loop fusion | flops 16646144 | bytes 17301504 | tf_op jit(solution)/shard_map/reduce_sum | solution.py:29
  602.9 0.1 add_divide_fusion.1
  603.1 0.0 copy-start
  603.1 16.0 %fusion.9 = (f32[16,8192]{1,0:T(8,128)S(1)}, f32[16,8192]{1,0:T(8,128)S(1)}) fusion(bf16[16,1,4,16,8192]{4,0,3,2,1:T(8,128)(2,1)} %bitcast.6, f32[16,8192]{1,0:T(8,128)S(1)} %get-tuple-element.14), kind=kLoop, calls=%fused_computation.10 | loop fusion | flops 83623936 | bytes 18350080 | tf_op jit(solution)/shard_map/reduce_sum | solution.py:30
  619.1 0.2 exponential_subtract_fusion
  619.3 0.4 div.23
  619.8 0.4 sqrt.7
  620.2 0.4 sub.60
  620.7 0.4 reshape.144
  621.1 2.7 reduce_window_sum.11
  623.9 1.0 fusion.16
  624.9 3.5 multiply_reduce_fusion.1
  628.3 1.1 stack.13
  629.4 1.1 stack.14
  630.6 0.2 stack.15
  630.8 0.2 sub.65
  630.9 0.5 maximum_multiply_fusion
  631.5 1.0 fusion.21
  632.5 0.3 copy.78
  632.8 1.5 collective-permute-start
  634.3 0.7 fusion.22
  636.3 10.0 %collective-permute-done = f32[4,4,8192]{2,1,0:T(4,128)S(1)} collective-permute-done((f32[4,4,8192]{2,1,0:T(4,128)S(1)}, f32[4,4,8192]{2,1,0:T(4,128)S(1)}, u32[]{:S(2)}, u32[]{:S(2)}) %collective-permute-start) | collective-permute-done | bytes 524320 | tf_op jit(solution)/shard_map/ppermute | solution.py:13
  646.4 0.7 broadcast_select_fusion.1
  647.1 0.7 multiply_add_fusion
  647.8 0.3 copy.52
  648.1 0.1 select_bitcast_fusion
  648.2 1.2 collective-permute-start.1
  650.6 4.6 collective-permute-done.1
  655.2 0.1 broadcast_select_fusion.2
  655.3 0.1 slice_subtract_fusion.1
  655.4 0.1 copy.79
  655.5 0.1 add_bitcast_fusion
  655.6 1.1 collective-permute-start.2
  658.1 4.9 collective-permute-done.2
  663.0 0.1 bitcast_select_fusion.2
  663.1 0.1 fusion.20
  663.2 0.8 copy.57
  (5 shorter events, 0.1 us)
Async XLA Ops:
  405.8 7.1 %copy-start.1 = (s32[1,64]{1,0:T(1,128)S(1)}, s32[1,64]{1,0:T(1,128)}, u32[]{:S(2)}) copy-start(s32[1,64]{1,0:T(1,128)} %param.4) | copy-start | bytes 772
  405.8 190.2 %all-to-all-start.1 = ((bf16[16,1,64,8192]{3,0,1,2:T(8,128)(2,1)}), bf16[16,1,64,8192]{3,0,1,2:T(8,128)(2,1)}, u32[]{:S(2)}, u32[]{:S(2)}) async-start(bf16[16,1,64,8192]{3,0,1,2:T(8,128)(2,1)} %copy.47), calls=%async_computation.1 | async-start | bytes 33554432 | tf_op jit(solution)/shard_map/all_to_all | solution.py:46
  603.1 31.3 %copy-start = (s32[8]{0:T(128)S(1)}, s32[8]{0:T(128)}, u32[]{:S(2)}) copy-start(s32[8]{0:T(128)} %param.5) | copy-start | bytes 100
  632.8 13.5 %collective-permute-start = (f32[4,4,8192]{2,1,0:T(4,128)S(1)}, f32[4,4,8192]{2,1,0:T(4,128)S(1)}, u32[]{:S(2)}, u32[]{:S(2)}) collective-permute-start(f32[4,4,8192]{2,1,0:T(4,128)S(1)} %bitcast.91), channel_id=1, source_target_pairs={{0,4},{4,0},{8,12},{12,8},{16,20},{20,16},{24,28},{28,24},{1,5},{5... | collective-permute-start | bytes 1572872 | tf_op jit(solution)/shard_map/ppermute | solution.py:13
  648.2 7.0 %collective-permute-start.1 = (f32[4,2,8192]{2,0,1:T(4,128)S(1)}, f32[4,2,8192]{2,0,1:T(4,128)S(1)}, u32[]{:S(2)}, u32[]{:S(2)}) collective-permute-start(f32[4,2,8192]{2,0,1:T(4,128)S(1)} %select_bitcast_fusion), channel_id=1, source_target_pairs={{0,8},{4,12},{8,0},{12,4},{16,24},{20,28},{24,16},{28,20},{1,9},{5... | collective-permute-start | bytes 786440 | tf_op jit(solution)/shard_map/ppermute | solution.py:13
  655.6 7.3 %collective-permute-start.2 = (f32[4,1,8192]{2,0,1:T(4,128)S(1)}, f32[4,1,8192]{2,0,1:T(4,128)S(1)}, u32[]{:S(2)}, u32[]{:S(2)}) collective-permute-start(f32[4,1,8192]{2,0,1:T(4,128)S(1)} %select_bitcast_fusion.1), channel_id=1, source_target_pairs={{0,16},{4,20},{8,24},{12,28},{16,0},{20,4},{24,8},{28,12},{1,17},{... | collective-permute-start | bytes 393224 | tf_op jit(solution)/shard_map/ppermute | solution.py:13
where the time goes:
time: 664 us
  blocking collectives  370 us (56%)
  waiting for transfers between devices  202 us (30%)
  local copies, waits for them, and re-layouts  42.9 us (6%)
  other arithmetic  34.2 us (5%)
  starting transfers between devices  10.9 us (2%)
    all_to_all x1, blocking collectives, body(): lax.all_to_all(ensemble, 'depth', split_axis=1, concat_axis=2, tiled=True)  370 us
    all_to_all x1, waiting for transfers between devices, body(): lax.all_to_all(lax.all_to_all(ensemble, 'depth', split_axis=1, concat_axi...  182 us
    all_to_all x2, local copies, waits for them, and re-layouts, body(): lax.all_to_all(ensemble, 'depth', split_axis=1, concat_axis=2, tiled=True)  27.3 us
    ppermute x3, waiting for transfers between devices, swapped(): lax.ppermute(x, axis, [(i, i ^ 1 << apart) for i in range(lax.axis_size(a...  19.5 us
    reduce_sum x1, other arithmetic, render_members(): variance = jnp.mean((samples - mean_field) ** 2, axis=0)  16 us
  transfers between devices with their start and end apart: 4, of which 4 were waited for; matrix products, arithmetic and copies ran while one was open for 0% of the time, Pallas kernels for 0%

commit v1 on v0

--- a/solution.py
+++ b/solution.py
@@ -43,12 +43,20 @@
     pixels = cells // BZ
     flag_row = active[0]
     own_flags = lax.dynamic_slice_in_dim(flag_row, tile_id * per_tile, per_tile).astype(jnp.float32)
-    regrouped = lax.all_to_all(
-        lax.all_to_all(ensemble, "depth", split_axis=1, concat_axis=2, tiled=True),
-        "tile",
-        split_axis=2,
-        concat_axis=0,
-        tiled=True,
+    regrouped = jnp.concatenate(
+        lax.all_to_all(
+            jnp.stack(
+                jnp.split(
+                    lax.all_to_all(ensemble, "depth", split_axis=1, concat_axis=2, tiled=True),
+                    lax.axis_size("tile"),
+                    axis=2,
+                )
+            ),
+            "tile",
+            0,
+            0,
+        ),
+        axis=0,
     )
     samples = regrouped.astype(jnp.float32).reshape(regrouped.shape[0], per_tile, BZ, pixels)
     shaded = render_members(samples) * own_flags[None, :, None]

time: 664 us -> 657 us (0.989)
  local copies, waits for them, and re-layouts: 42.9 us -> 23.7 us
  other arithmetic: 34.2 us -> 45.5 us
    all_to_all x2 -> x1, local copies, waits for them, and re-layouts: 27.3 us -> 2.18 us  [body(): lax.all_to_all(ensemble, 'depth', split_axis=1, concat_axis=2, tiled=True)]
    another operation x0 -> x1, other arithmetic: none -> 13.8 us  [body(): jnp.stack(jnp.split(lax.all_to_all(ensemble, 'depth', split_axis=1, conca...]
where the time goes in v1:
time: 657 us; the launch traced here: 656 us
  blocking collectives  370 us (56%)
  waiting for transfers between devices  202 us (31%)
  other arithmetic  45.5 us (7%)
  local copies, waits for them, and re-layouts  23.7 us (4%)
  starting transfers between devices  10.9 us (2%)
    all_to_all x1, blocking collectives, body(): lax.all_to_all(ensemble, 'depth', split_axis=1, concat_axis=2, tiled=True)  370 us
    all_to_all x1, waiting for transfers between devices, body(): lax.all_to_all(jnp.stack(jnp.split(lax.all_to_all(ensemble, 'depth', spli...  182 us
    ppermute x3, waiting for transfers between devices, swapped(): lax.ppermute(x, axis, [(i, i ^ 1 << apart) for i in range(lax.axis_size(a...  19.5 us
    another operation x1, other arithmetic, body(): jnp.stack(jnp.split(lax.all_to_all(ensemble, 'depth', split_axis=1, conca...  13.8 us
    reduce_sum x1, other arithmetic, render_members(): variance = jnp.mean((samples - mean_field) ** 2, axis=0)  13.7 us
  transfers between devices with their start and end apart: 4, of which 4 were waited for; matrix products, arithmetic and copies ran while one was open for 0% of the time, Pallas kernels for 0%

profile of v1, /device:TPU:0, one launch (start us, length us, event | category | flops | bytes accessed | tf_op | source)
XLA Modules:
  0.0 656.0 jit_solution(14176643432243912178)
XLA Ops:
  0.0 8.5 %copy.48 = bf16[16,8,8,8192]{3,2,0,1:T(8,128)(2,1)S(1)} copy(bf16[16,8,8,8192]{3,2,1,0:T(8,128)(2,1)} %param.3) | data formatting | bytes 33554432 | tf_op args[0]
  8.5 369.9 %all_to_all.17 = bf16[16,8,8,8192]{3,2,0,1:T(8,128)(2,1)S(1)} all-to-all(bf16[16,8,8,8192]{3,2,0,1:T(8,128)(2,1)S(1)} %copy.48), channel_id=1, replica_groups=mesh['depth'=8,'tile'=4] {'depth'}, dimensions={1} | all-to-all | bytes 33554432 | tf_op jit(solution)/shard_map/all_to_all | solution.py:50
  378.4 2.2 copy.79
  380.6 5.9 slice_bitcast_fusion.3
  386.5 13.8 %pad_maximum_fusion = bf16[4,16,1,16,8192]{4,3,1,2,0:T(8,128)(2,1)} fusion(bf16[1,16,1,16,8192]{4,3,1,2,0:T(8,128)(2,1)} %get-tuple-element.11, bf16[1,16,1,16,8192]{4,3,1,2,0:T(8,128)(2,1)} %get-tuple-element.12, bf16[1,16,1,16,8192]{4,3,1,2,0:T(8,128)(2,1)} %get-tuple-element.13, bf16[1,16,1,16,8192]{4,3,1,2,0:T(8,128)(2,1)} %get-tuple-element.10), kind=kLoop, calls=%fused_computation.11 | loop fusion | flops 25165824 | bytes 33554432 | tf_op jit(solution)/shard_map/stack | solution.py:48
  400.3 7.1 %all-to-all-start.1 = ((bf16[4,16,1,16,8192]{4,3,1,2,0:T(8,128)(2,1)}), bf16[4,16,1,16,8192]{4,3,1,2,0:T(8,128)(2,1)}, u32[]{:S(2)}, u32[]{:S(2)}) async-start(bf16[4,16,1,16,8192]{4,3,1,2,0:T(8,128)(2,1)} %pad_maximum_fusion), calls=%async_computation.1 | async-start | bytes 33554432 | tf_op jit(solution)/shard_map/all_to_all | solution.py:47
  407.4 0.1 convert_reduce_fusion.1
  407.5 0.1 convert_element_type.21
  407.6 0.1 mul.110
  407.8 0.3 mul.111
  408.1 182.4 %all-to-all-done.1 = bf16[4,16,1,16,8192]{4,3,1,2,0:T(8,128)(2,1)} async-done(((bf16[4,16,1,16,8192]{4,3,1,2,0:T(8,128)(2,1)}), bf16[4,16,1,16,8192]{4,3,1,2,0:T(8,128)(2,1)}, u32[]{:S(2)}, u32[]{:S(2)}) %all-to-all-start.1) | async-done | bytes 16777248 | tf_op jit(solution)/shard_map/all_to_all | solution.py:47
  590.5 6.8 %convert_reduce_fusion = f32[16,8192]{1,0:T(8,128)S(1)} fusion(bf16[4,16,1,16,8192]{4,3,1,2,0:T(8,128)(2,1)} %all-to-all-done.1), kind=kLoop, calls=%fused_computation.1 | loop fusion | flops 16646144 | bytes 17301504 | tf_op jit(solution)/shard_map/reduce_sum | solution.py:29
  597.2 0.1 add_divide_fusion.1
  597.4 0.0 copy-start
  597.4 13.7 %fusion.6 = (f32[16,8192]{1,0:T(8,128)S(1)}, f32[16,8192]{1,0:T(8,128)S(1)}) fusion(bf16[4,16,1,16,8192]{4,3,1,2,0:T(8,128)(2,1)} %all-to-all-done.1, f32[16,8192]{1,0:T(8,128)S(1)} %get-tuple-element.18), kind=kLoop, calls=%fused_computation.9 | loop fusion | flops 83623936 | bytes 18350080 | tf_op jit(solution)/shard_map/reduce_sum | solution.py:30
  611.2 0.2 exponential_subtract_fusion
  611.4 0.4 div.23
  611.9 0.4 sqrt.7
  612.3 0.4 sub.60
  612.8 0.4 reshape.143
  613.2 2.7 reduce_window_sum.11
  615.9 1.0 fusion.13
  616.9 3.5 multiply_reduce_fusion.1
  620.4 1.1 stack.33
  621.5 1.1 stack.34
  622.6 0.2 stack.35
  622.8 0.2 sub.65
  623.0 0.5 maximum_multiply_fusion
  623.5 1.0 fusion.18
  624.5 0.3 copy.80
  624.9 1.5 collective-permute-start
  626.4 0.7 fusion.19
  628.4 10.0 %collective-permute-done = f32[4,4,8192]{2,1,0:T(4,128)S(1)} collective-permute-done((f32[4,4,8192]{2,1,0:T(4,128)S(1)}, f32[4,4,8192]{2,1,0:T(4,128)S(1)}, u32[]{:S(2)}, u32[]{:S(2)}) %collective-permute-start) | collective-permute-done | bytes 524320 | tf_op jit(solution)/shard_map/ppermute | solution.py:13
  638.4 0.7 broadcast_select_fusion.1
  639.1 0.7 multiply_add_fusion
  639.8 0.3 copy.54
  640.2 0.1 select_bitcast_fusion
  640.3 1.2 collective-permute-start.1
  642.7 4.6 collective-permute-done.1
  647.3 0.1 broadcast_select_fusion.2
  647.4 0.1 slice_subtract_fusion.1
  647.5 0.1 copy.81
  647.5 0.1 add_bitcast_fusion
  647.7 1.1 collective-permute-start.2
  650.2 4.9 collective-permute-done.2
  655.0 0.1 bitcast_select_fusion.2
  655.2 0.1 fusion.17
  655.2 0.8 copy.59
  (6 shorter events, 0.1 us)
Async XLA Ops:
  400.3 7.1 %copy-start.1 = (s32[1,64]{1,0:T(1,128)S(1)}, s32[1,64]{1,0:T(1,128)}, u32[]{:S(2)}) copy-start(s32[1,64]{1,0:T(1,128)} %param.4) | copy-start | bytes 772
  400.3 190.1 %all-to-all-start.1 = ((bf16[4,16,1,16,8192]{4,3,1,2,0:T(8,128)(2,1)}), bf16[4,16,1,16,8192]{4,3,1,2,0:T(8,128)(2,1)}, u32[]{:S(2)}, u32[]{:S(2)}) async-start(bf16[4,16,1,16,8192]{4,3,1,2,0:T(8,128)(2,1)} %pad_maximum_fusion), calls=%async_computation.1 | async-start | bytes 33554432 | tf_op jit(solution)/shard_map/all_to_all | solution.py:47
  597.4 29.0 %copy-start = (s32[8]{0:T(128)S(1)}, s32[8]{0:T(128)}, u32[]{:S(2)}) copy-start(s32[8]{0:T(128)} %param.5) | copy-start | bytes 100
  624.9 13.5 %collective-permute-start = (f32[4,4,8192]{2,1,0:T(4,128)S(1)}, f32[4,4,8192]{2,1,0:T(4,128)S(1)}, u32[]{:S(2)}, u32[]{:S(2)}) collective-permute-start(f32[4,4,8192]{2,1,0:T(4,128)S(1)} %bitcast.73), channel_id=1, source_target_pairs={{0,4},{4,0},{8,12},{12,8},{16,20},{20,16},{24,28},{28,24},{1,5},{5... | collective-permute-start | bytes 1572872 | tf_op jit(solution)/shard_map/ppermute | solution.py:13
  640.3 7.0 %collective-permute-start.1 = (f32[4,2,8192]{2,0,1:T(4,128)S(1)}, f32[4,2,8192]{2,0,1:T(4,128)S(1)}, u32[]{:S(2)}, u32[]{:S(2)}) collective-permute-start(f32[4,2,8192]{2,0,1:T(4,128)S(1)} %select_bitcast_fusion), channel_id=1, source_target_pairs={{0,8},{4,12},{8,0},{12,4},{16,24},{20,28},{24,16},{28,20},{1,9},{5... | collective-permute-start | bytes 786440 | tf_op jit(solution)/shard_map/ppermute | solution.py:13
  647.7 7.3 %collective-permute-start.2 = (f32[4,1,8192]{2,0,1:T(4,128)S(1)}, f32[4,1,8192]{2,0,1:T(4,128)S(1)}, u32[]{:S(2)}, u32[]{:S(2)}) collective-permute-start(f32[4,1,8192]{2,0,1:T(4,128)S(1)} %select_bitcast_fusion.1), channel_id=1, source_target_pairs={{0,16},{4,20},{8,24},{12,28},{16,0},{20,4},{24,8},{28,12},{1,17},{... | collective-permute-start | bytes 393224 | tf_op jit(solution)/shard_map/ppermute | solution.py:13
